TPU v7x, 256 devices: a whole 4x4x8 slice. The times are simulated.
256 devices in a mesh: dp: 64 (over y, x_lo, z), pair: 4 (over x_hi, core).
Axes of the slice: x: 4 (x_hi: 2, x_lo: 2; x = x_hi * 2 + x_lo), y: 4, z: 8, core: 2. Of those that a mesh axis runs over, the one named last changes fastest.
Arguments:
- student_image: bfloat16 [65536, 512], P(('dp', 'pair')), may hold values from -60 to 60
- student_text: bfloat16 [65536, 512], P(('dp', 'pair')), may hold values from -6 to 6
- teacher_image: bfloat16 [65536, 1280], P(('dp', 'pair')), may hold values from -60 to 60
- teacher_text: bfloat16 [65536, 1280], P(('dp', 'pair')), may hold values from -6 to 6
Outputs:
- grad_image: float32 [65536, 512], P(('dp', 'pair'))
- grad_text: float32 [65536, 512], P(('dp', 'pair'))
All inputs are finite; a program needn't handle non-finite values.
Results may differ from a plain program's by a relative error of at most 0.0025.
Values may be sent and summed in bfloat16 or wider, within the bound.
A program may use at most 128 MiB of HBM per device.

v0:
```python
import math

import jax
import jax.numpy as jnp
from jax import lax
from jax.sharding import PartitionSpec as P

WINDOW = 4


def from_behind(value, axis, steps):
    count = lax.axis_size(axis)
    pairs = [(source, (source + steps) % count) for source in range(count)]
    return lax.ppermute(value, axis, pairs)


def combined_all(value, axis, join):
    pieces = jax.tree.map(lambda part: lax.all_gather(part, axis), value)
    head = jax.tree.map(lambda part: part[0], pieces)
    tail = jax.tree.map(lambda part: part[1:], pieces)
    subtotal, _ = lax.scan(lambda subtotal, section: (join(subtotal, section), None), head, tail)
    return subtotal


def stats_of(scores, axis):
    top = jnp.max(scores, axis=axis)
    total = jnp.sum(jnp.exp(scores - jnp.expand_dims(top, axis)), axis=axis)
    return (top, total)


def combine_stats(first, second):
    result = []
    for offset in (0, 2):
        top = jnp.maximum(first[offset], second[offset])
        total = first[offset + 1] * jnp.exp(first[offset] - top) + second[offset + 1] * jnp.exp(
            second[offset] - top
        )
        result += [top, total]
    return tuple(result)


def as_tuple(stacked):
    return (stacked[0], stacked[1], stacked[2], stacked[3])


def weight_tile(s_tile, t_tile, row_stats, col_stats):
    rm_s, rz_s, rm_t, rz_t = row_stats
    cm_s, cz_s, cm_t, cz_t = col_stats
    return (
        jnp.exp(s_tile - rm_s[:, None]) / rz_s[:, None]
        - jnp.exp(t_tile - rm_t[:, None]) / rz_t[:, None]
        + jnp.exp(s_tile - cm_s[None, :]) / cz_s[None, :]
        - jnp.exp(t_tile - cm_t[None, :]) / cz_t[None, :]
    ).astype(jnp.bfloat16)


def on_device(student_image, student_text, teacher_image, teacher_text):
    width_s = student_image.shape[1]
    scale_s = 2.0 / math.sqrt(width_s)
    scale_t = 2.0 / math.sqrt(teacher_image.shape[1])
    shard_len = student_image.shape[0]
    block_len = shard_len * lax.axis_size("pair")
    both_text = jnp.concatenate([student_text, teacher_text], axis=1)
    image_s, image_t = (student_image, teacher_image)
    own_block = lax.all_gather(both_text, "pair", axis=0, tiled=True)
    blocks = [own_block]
    for step in range(1, WINDOW):
        blocks.append(from_behind(own_block, "dp", -step))
    partners = jnp.concatenate(blocks, axis=0)
    part_s = partners[:, :width_s]
    part_t = partners[:, width_s:]
    dims = (((1,), (1,)), ((), ()))
    s_tile = lax.dot_general(image_s, part_s, dims, preferred_element_type=jnp.float32) * scale_s
    t_tile = lax.dot_general(image_t, part_t, dims, preferred_element_type=jnp.float32) * scale_t
    row_stats = stats_of(s_tile, 1) + stats_of(t_tile, 1)
    col_local = stats_of(s_tile, 0) + stats_of(t_tile, 0)
    col_block = combined_all(col_local, "pair", combine_stats)
    stacked = jnp.stack(col_block, axis=0).reshape(4, WINDOW, block_len)
    home = as_tuple(stacked[:, 0])
    for step in range(1, WINDOW):
        arrived = from_behind(stacked[:, step], "dp", step)
        home = combine_stats(home, as_tuple(arrived))
    home_all = jnp.stack(home, axis=0)
    pieces = [home_all]
    for step in range(1, WINDOW):
        pieces.append(from_behind(home_all, "dp", -step))
    band_stats = jnp.concatenate(pieces, axis=1)
    col_stats = as_tuple(band_stats)
    weights = weight_tile(s_tile, t_tile, row_stats, col_stats)
    image_terms = jnp.dot(weights, part_s, preferred_element_type=jnp.float32)
    text_part = lax.dot_general(
        weights, image_s, (((0,), (0,)), ((), ())), preferred_element_type=jnp.float32
    )
    grad_image = image_terms * scale_s
    text_home = text_part[:block_len]
    for step in range(1, WINDOW):
        text_home = text_home + from_behind(
            text_part[step * block_len : (step + 1) * block_len], "dp", step
        )
    grad_text = lax.psum_scatter(text_home, "pair", scatter_dimension=0, tiled=True) * scale_s
    return (grad_image, grad_text)


def solution(mesh):
    return jax.shard_map(
        on_device,
        mesh=mesh,
        in_specs=(
            P(("dp", "pair"), None),
            P(("dp", "pair"), None),
            P(("dp", "pair"), None),
            P(("dp", "pair"), None),
        ),
        out_specs=(P(("dp", "pair"), None), P(("dp", "pair"), None)),
        check_vma=False,
    )
```

profile of v0, /device:TPU:1, one launch (start us, length us, event | category | flops | bytes accessed | tf_op | source)
XLA Modules:
  0.0 925.9 jit_solution(9770478895423489893)
XLA Ops:
  7.2 2.2 pad_maximum_fusion
  9.5 42.7 %all-gather.6.cloned.1.call-done = bf16[1024,1792]{1,0:T(8,128)(2,1)} async-done(((bf16[256,1792]{1,0:T(8,128)(2,1)}), bf16[1024,1792]{1,0:T(8,128)(2,1)}) %all-gather.6.cloned.1.call-update) | async-done | bytes 3670032 | tf_op jit(solution)/shard_map/all_gather | solution.py:65
  52.2 5.2 collective-permute-start
  57.4 1.9 collective-permute-start.1
  60.2 2.3 constant_dynamic-update-slice_fusion.3
  62.5 152.9 %collective-permute-done = bf16[1024,1792]{1,0:T(8,128)(2,1)} collective-permute-done((bf16[1024,1792]{1,0:T(8,128)(2,1)}, bf16[1024,1792]{1,0:T(8,128)(2,1)}, u32[]{:S(2)}, u32[]{:S(2)}) %collective-permute-start) | collective-permute-done | bytes 3670048 | tf_op jit(solution)/shard_map/ppermute | solution.py:14
  215.4 2.3 constant_dynamic-update-slice_fusion.2
  217.7 84.0 %collective-permute-done.1 = bf16[1024,1792]{1,0:T(8,128)(2,1)} collective-permute-done((bf16[1024,1792]{1,0:T(8,128)(2,1)}, bf16[1024,1792]{1,0:T(8,128)(2,1)}, u32[]{:S(2)}, u32[]{:S(2)}) %collective-permute-start.1) | collective-permute-done | bytes 3670048 | tf_op jit(solution)/shard_map/ppermute | solution.py:14
  301.7 2.3 constant_dynamic-update-slice_fusion.1
  304.0 225.4 %collective-permute-done.2 = bf16[1024,1792]{1,0:T(8,128)(2,1)} collective-permute-done((bf16[1024,1792]{1,0:T(8,128)(2,1)}, bf16[1024,1792]{1,0:T(8,128)(2,1)}, u32[]{:S(2)}, u32[]{:S(2)}) %collective-permute-start.2) | collective-permute-done | bytes 3670048 | tf_op jit(solution)/shard_map/ppermute | solution.py:14
  529.4 2.3 constant_dynamic-update-slice_fusion
  531.7 3.0 fusion.30
  536.5 7.7 all-gather.3
  545.6 2.0 copy-done.3
  547.6 1.9 fusion.6
  549.5 6.7 all-gather.1
  556.2 6.7 all-gather
  563.0 6.7 all-gather.2
  570.6 2.8 collective-permute-start.4
  573.4 2.6 collective-permute-start.5
  578.6 3.5 collective-permute-done.5
  583.4 2.0 collective-permute-start.7
  585.4 5.1 collective-permute-start.8
  591.5 7.4 subtract_convert_fusion
  601.0 4.6 collective-permute-start.11
  605.6 94.2 %collective-permute-done.10 = f32[1024,512]{1,0:T(8,128)S(1)} collective-permute-done((f32[1024,512]{1,0:T(8,128)S(1)}, f32[1024,512]{1,0:T(8,128)S(1)}, u32[]{:S(2)}, u32[]{:S(2)}) %collective-permute-start.10) | collective-permute-done | bytes 2097184 | tf_op jit(solution)/shard_map/ppermute | solution.py:14
  699.8 131.3 %collective-permute-done.11 = f32[1024,512]{1,0:T(8,128)S(1)} collective-permute-done((f32[1024,512]{1,0:T(8,128)S(1)}, f32[1024,512]{1,0:T(8,128)S(1)}, u32[]{:S(2)}, u32[]{:S(2)}) %collective-permute-start.11) | collective-permute-done | bytes 2097184 | tf_op jit(solution)/shard_map/ppermute | solution.py:14
  831.1 44.4 %collective-permute-done.9 = f32[1024,512]{1,0:T(8,128)S(1)} collective-permute-done((f32[1024,512]{1,0:T(8,128)S(1)}, f32[1024,512]{1,0:T(8,128)S(1)}, u32[]{:S(2)}, u32[]{:S(2)}) %collective-permute-start.9) | collective-permute-done | bytes 2097184 | tf_op jit(solution)/shard_map/ppermute | solution.py:14
  875.5 2.3 fusion.11
  877.9 4.3 fusion.12
  882.2 35.0 %reduce-scatter.2.cloned.1.call-done = f32[256,512]{1,0:T(8,128)} async-done(((f32[1024,512]{1,0:T(8,128)}), f32[256,512]{1,0:T(8,128)}) %reduce-scatter.2.cloned.1.call-update) | async-done | bytes 524304 | tf_op jit(solution)/shard_map/reduce_scatter | solution.py:100
  917.1 1.9 broadcast_multiply_fusion
  (77 shorter events, 12.2 us)
Async XLA Ops:
  7.2 524.5 %copy-start = (bf16[256,1280]{1,0:T(8,128)(2,1)S(1)}, bf16[256,1280]{1,0:T(8,128)(2,1)}, u32[]{:S(2)}) copy-start(bf16[256,1280]{1,0:T(8,128)(2,1)} %param.8) | copy-start | bytes 1966084
  7.2 45.0 %all-gather.6.cloned.1.call-start = ((), (), s32[]{:S(2)}) async-start(), calls=%async_computation.1 | async-start | bytes 4587520 | tf_op jit(solution)/shard_map/all_gather | solution.py:65
  9.5 907.7 %reduce-scatter.2.cloned.1.call-start = ((), (), s32[]{:S(2)}) async-start(), calls=%async_computation.2 | async-start | bytes 2621440 | tf_op jit(solution)/shard_map/reduce_scatter | solution.py:100
  52.2 163.3 %collective-permute-start = (bf16[1024,1792]{1,0:T(8,128)(2,1)}, bf16[1024,1792]{1,0:T(8,128)(2,1)}, u32[]{:S(2)}, u32[]{:S(2)}) collective-permute-start(bf16[1024,1792]{1,0:T(8,128)(2,1)} %all-gather.6.cloned.1.call-done), channel_id=1, source_target_pairs={{0,252},{4,0},{8,4},{12,8},{16,12},{20,16},{24,20},{28,24},{32,28}... | collective-permute-start | bytes 11010056 | tf_op jit(solution)/shard_map/ppermute | solution.py:14
  57.4 244.3 %collective-permute-start.1 = (bf16[1024,1792]{1,0:T(8,128)(2,1)}, bf16[1024,1792]{1,0:T(8,128)(2,1)}, u32[]{:S(2)}, u32[]{:S(2)}) collective-permute-start(bf16[1024,1792]{1,0:T(8,128)(2,1)} %all-gather.6.cloned.1.call-done), channel_id=1, source_target_pairs={{0,248},{4,252},{8,0},{12,4},{16,8},{20,12},{24,16},{28,20},{32,24... | collective-permute-start | bytes 11010056 | tf_op jit(solution)/shard_map/ppermute | solution.py:14
  59.3 470.1 %collective-permute-start.2 = (bf16[1024,1792]{1,0:T(8,128)(2,1)}, bf16[1024,1792]{1,0:T(8,128)(2,1)}, u32[]{:S(2)}, u32[]{:S(2)}) collective-permute-start(bf16[1024,1792]{1,0:T(8,128)(2,1)} %all-gather.6.cloned.1.call-done), channel_id=1, source_target_pairs={{0,244},{4,248},{8,252},{12,0},{16,4},{20,8},{24,12},{28,16},{32,2... | collective-permute-start | bytes 11010056 | tf_op jit(solution)/shard_map/ppermute | solution.py:14
  531.7 12.5 %copy-start.4 = (bf16[4096,1792]{1,0:T(8,128)(2,1)}, bf16[4096,1792]{1,0:T(8,128)(2,1)S(1)}, u32[]{:S(2)}) copy-start(bf16[4096,1792]{1,0:T(8,128)(2,1)S(1)} %constant_dynamic-update-slice_fusion) | copy-start | bytes 44040196
  534.7 10.9 %copy-start.2 = (f32[4096,256]{1,0:T(8,128)}, f32[4096,256]{1,0:T(8,128)S(1)}, u32[]{:S(2)}) copy-start(f32[4096,256]{1,0:T(8,128)S(1)} %get-tuple-element.105) | copy-start | bytes 12582916
  534.7 9.5 %copy-start.6 = (bf16[256,512]{1,0:T(8,128)(2,1)S(1)}, bf16[256,512]{1,0:T(8,128)(2,1)}, u32[]{:S(2)}) copy-start(bf16[256,512]{1,0:T(8,128)(2,1)} %param.6) | copy-start | bytes 786436
  544.2 1.4 copy-start.5
  545.6 2.0 copy-start.3
  545.6 24.1 %slice-start = ((f32[16384]{0:T(1024)}), f32[12288]{0:T(1024)S(1)}, s32[]{:S(2)}) async-start(f32[16384]{0:T(1024)} %copy-done.5), calls=%async_computation.3 | async-start | bytes 98304 | tf_op jit(solution)/shard_map/slice | solution.py:20
  545.6 24.2 %slice-start.1 = ((f32[16384]{0:T(1024)}), f32[4096]{0:T(1024)S(1)}, s32[]{:S(2)}) async-start(f32[16384]{0:T(1024)} %copy-done.5), calls=%async_computation.4 | async-start | bytes 32768 | tf_op jit(solution)/shard_map/slice | solution.py:19
  570.5 6.9 collective-permute-start.3
  570.6 8.0 collective-permute-start.4
  573.4 8.7 collective-permute-start.5
  582.2 8.3 collective-permute-start.6
  583.4 7.2 collective-permute-start.7
  585.4 6.0 collective-permute-start.8
  600.9 98.9 %collective-permute-start.10 = (f32[1024,512]{1,0:T(8,128)S(1)}, f32[1024,512]{1,0:T(8,128)S(1)}, u32[]{:S(2)}, u32[]{:S(2)}) collective-permute-start(f32[1024,512]{1,0:T(8,128)S(1)} %get-tuple-element.94), channel_id=1, source_target_pairs={{0,8},{4,12},{8,16},{12,20},{16,24},{20,28},{24,32},{28,36},{32,40... | collective-permute-start | bytes 6291464 | tf_op jit(solution)/shard_map/ppermute | solution.py:14
  601.0 230.1 %collective-permute-start.11 = (f32[1024,512]{1,0:T(8,128)S(1)}, f32[1024,512]{1,0:T(8,128)S(1)}, u32[]{:S(2)}, u32[]{:S(2)}) collective-permute-start(f32[1024,512]{1,0:T(8,128)S(1)} %get-tuple-element.93), channel_id=1, source_target_pairs={{0,12},{4,16},{8,20},{12,24},{16,28},{20,32},{24,36},{28,40},{32,4... | collective-permute-start | bytes 6291464 | tf_op jit(solution)/shard_map/ppermute | solution.py:14
  605.6 269.9 %collective-permute-start.9 = (f32[1024,512]{1,0:T(8,128)S(1)}, f32[1024,512]{1,0:T(8,128)S(1)}, u32[]{:S(2)}, u32[]{:S(2)}) collective-permute-start(f32[1024,512]{1,0:T(8,128)S(1)} %get-tuple-element.92), channel_id=1, source_target_pairs={{0,4},{4,8},{8,12},{12,16},{16,20},{20,24},{24,28},{28,32},{32,36}... | collective-permute-start | bytes 6291464 | tf_op jit(solution)/shard_map/ppermute | solution.py:14
  877.8 41.2 %copy-start.1 = (bf16[256,1280]{1,0:T(8,128)(2,1)S(1)}, bf16[256,1280]{1,0:T(8,128)(2,1)}, u32[]{:S(2)}) copy-start(bf16[256,1280]{1,0:T(8,128)(2,1)} %param.8) | copy-start | bytes 1966084
Sparse Core Ops, SparseCore 0:
  9.8 42.2 all-gather.5
  878.0 39.1 reduce-scatter.1
where the time goes:
time: 926 us
  waiting for transfers between devices  817 us (88%)
  blocking collectives  27.9 us (3%)
  starting transfers between devices  26.6 us (3%)
  other arithmetic  17.7 us (2%)
  between operations  14.3 us (2%)
  local copies, waits for them, and re-layouts  12.4 us (1%)
  matrix products  9.95 us (1%)
    ppermute x12, waiting for transfers between devices, from_behind(): return lax.ppermute(value, axis, pairs)  739 us
    all_gather x1, waiting for transfers between devices, on_device(): own_block = lax.all_gather(both_text, 'pair', axis=0, tiled=True)  42.7 us
    reduce_scatter x1, waiting for transfers between devices, on_device(): lax.psum_scatter(text_home, 'pair', scatter_dimension=0, tiled=True)  35 us
    all_gather x4, blocking collectives, combined_all(): pieces = jax.tree.map(lambda part: lax.all_gather(part, axis), value)  27.9 us
    ppermute x12, starting transfers between devices, from_behind(): return lax.ppermute(value, axis, pairs)  26.5 us
  transfers between devices with their start and end apart: 14, of which 12 were waited for; matrix products, arithmetic and copies ran while one was open for 1% of the time, Pallas kernels for 0%

commit v1 on v0

v1 whole, which is shorter than its diff:
```python
import functools
import math

import jax
import jax.numpy as jnp
from jax import lax
from jax.experimental import pallas as pl
from jax.experimental.pallas import tpu as pltpu
from jax.sharding import PartitionSpec as P

MESH = pl.DeviceIdType.MESH
F32 = jnp.float32
BF16 = jnp.bfloat16

WINDOW = 4
PAIR = 4
ROWS = 256
BLOCK = ROWS * PAIR
CHUNKS = 2
CR = ROWS // CHUNKS
TILES = WINDOW * CHUNKS
SLAB = 32
SHIFTS = (-3, -2, -1, 1, 2, 3)
NT = (((1,), (1,)), ((), ()))
NN = (((1,), (0,)), ((), ()))
TN = (((0,), (0,)), ((), ()))


def rows_of(start, size):
    return pl.ds(pl.multiple_of(start, size), size)


def kernel(
    groups, scale_s, scale_t,
    si, st, ti, tt, out_image, out_text,
    img_s, img_t, txt_s, txt_t,
    s_buf, t_buf, e_img_s, e_img_t, e_txt_s, e_txt_t, w,
    istat, ist, rist, tcol, tst, rts, tsct, tsc, asc,
    g_send, g_recv, p_own, gi, gi_sib, gi_x, gi_sum,
    local_sem, tx_send, tx_recv, im_send, im_recv,
    ts_send, ts_recv, is_send, is_recv, g_ssem, g_rsem, gi_ssem, gi_rsem,
):
    d = lax.axis_index("dp")
    p = lax.axis_index("pair")
    sib = p + 1 - 2 * lax.rem(p, 2)
    far = lax.rem(p + 2, PAIR)
    diag = 3 - p
    mates = {1: sib, 2: far, 3: diag}

    def at(shift):
        return (lax.rem(d + shift + groups, groups), p)

    def remote(src, dst, ssem, rsem, device):
        return pltpu.make_async_remote_copy(
            src_ref=src, dst_ref=dst, send_sem=ssem, recv_sem=rsem,
            device_id=device, device_id_type=MESH,
        )

    own_rows = rows_of(p * ROWS, ROWS)
    locals_ = [
        pltpu.make_async_copy(st, txt_s.at[pl.ds(0, ROWS)], local_sem.at[0]),
        pltpu.make_async_copy(tt, txt_t.at[pl.ds(0, ROWS)], local_sem.at[1]),
        pltpu.make_async_copy(si, img_s.at[own_rows], local_sem.at[2]),
        pltpu.make_async_copy(ti, img_t.at[own_rows], local_sem.at[3]),
    ]
    for copy in locals_:
        copy.start()

    barrier = pltpu.get_barrier_semaphore()
    for shift in SHIFTS:
        pl.semaphore_signal(barrier, inc=1, device_id=at(shift), device_id_type=MESH)
    for r in (1, 2, 3):
        pl.semaphore_signal(barrier, inc=1, device_id=(d, mates[r]), device_id_type=MESH)
    for copy in locals_:
        copy.wait()
    pl.semaphore_wait(barrier, 9)

    def text_copies(n):
        here, there = pl.ds(n * CR, CR), pl.ds((n + CHUNKS) * CR, CR)
        return [
            remote(buf.at[here], buf.at[there], tx_send.at[i, n], tx_recv.at[i, n], at(-1))
            for i, buf in enumerate((txt_s, txt_t))
        ]

    def send_text(n):
        for copy in text_copies(n):
            copy.start()

    def text_arrives(n):
        for copy in text_copies(n - CHUNKS):
            copy.wait_recv()

    def image_copies(slot, quarter, device):
        rows = rows_of(quarter * ROWS, ROWS)
        return [
            remote(buf.at[rows], buf.at[rows], im_send.at[i, slot], im_recv.at[i, slot], device)
            for i, buf in enumerate((img_s, img_t))
        ]

    to_far = image_copies(0, p, (d, far))
    to_sib = image_copies(1, p, (d, sib))
    pass_on = image_copies(2, far, (d, sib))
    for copy in to_far + to_sib:
        copy.start()
    for n in range(CHUNKS):
        send_text(n)
    for n in range(CHUNKS, 2 * CHUNKS):
        text_arrives(n)
        send_text(n)
    for copy in to_far:
        copy.wait_recv()
    for copy in pass_on:
        copy.start()
    for copy in to_sib + pass_on:
        copy.wait_recv()

    tcol[...] = jnp.zeros_like(tcol)
    ist[...] = jnp.zeros_like(ist)
    tsct[...] = jnp.zeros_like(tsct)

    def tile_stats(j, buf, e_img, e_txt, which):
        base = j * CR

        def by_text(g, top):
            x = buf[rows_of(g * SLAB, SLAB), :]
            m = jnp.max(x, axis=1, keepdims=True)
            e = jnp.exp(x - m)
            rows = rows_of(base + g * SLAB, SLAB)
            e_txt[rows, :] = e
            tcol[rows, which : which + 1] = m
            tcol[rows, which + 2 : which + 3] = jnp.sum(e, axis=1, keepdims=True)
            return jnp.maximum(top, jnp.max(x.reshape(SLAB // 8, 8, BLOCK), axis=0))

        top = lax.fori_loop(0, CR // SLAB, by_text, jnp.full((8, BLOCK), -jnp.inf, F32))
        top = jnp.max(top, axis=0, keepdims=True)

        def by_image(g, total):
            e = jnp.exp(buf[rows_of(g * SLAB, SLAB), :] - top)
            e_img[rows_of(base + g * SLAB, SLAB), :] = e
            return total + jnp.sum(e.reshape(SLAB // 8, 8, BLOCK), axis=0)

        total = lax.fori_loop(0, CR // SLAB, by_image, jnp.zeros((8, BLOCK), F32))
        istat[which, pl.ds(j, 1), :] = top
        istat[which + 2, pl.ds(j, 1), :] = jnp.sum(total, axis=0, keepdims=True)

    def tile(j, carry):
        for n in range(2 * CHUNKS, 3 * CHUNKS):
            @pl.when(j == 2 * (n - 2 * CHUNKS + 1))
            def _(n=n):
                text_arrives(n)
                send_text(n)
        for n in range(3 * CHUNKS, 4 * CHUNKS):
            @pl.when(j == n)
            def _(n=n):
                text_arrives(n)
        rows = rows_of(j * CR, CR)
        s_buf[...] = lax.dot_general(txt_s[rows, :], img_s[...], NT, preferred_element_type=F32) * scale_s
        t_buf[...] = lax.dot_general(txt_t[rows, :], img_t[...], NT, preferred_element_type=F32) * scale_t
        tile_stats(j, s_buf, e_img_s, e_txt_s, 0)
        tile_stats(j, t_buf, e_img_t, e_txt_t, 1)
        return carry

    lax.fori_loop(0, TILES, tile, 0)

    tst[...] = jnp.transpose(tcol[...])[0:8, :]

    def text_stat_copy(i):
        shift = SHIFTS[i]
        low, high = max(0, shift), min(WINDOW, WINDOW + shift)
        size = (high - low) * ROWS
        return remote(
            tst.at[:, pl.ds(low * ROWS, size)], rts.at[i, :, pl.ds((low - shift) * ROWS, size)],
            ts_send.at[i], ts_recv.at[i], at(shift),
        )

    for i in range(6):
        text_stat_copy(i).start()

    for which in (0, 1):
        tops, totals = istat[which], istat[which + 2]
        top = jnp.max(tops, axis=0, keepdims=True)
        ist[which : which + 1, :] = top
        ist[which + 2 : which + 3, :] = jnp.sum(totals * jnp.exp(tops - top), axis=0, keepdims=True)

    def image_stat_copy(r):
        return remote(ist, rist.at[r - 1], is_send.at[r - 1], is_recv.at[r - 1], (d, mates[r]))

    for r in (1, 2, 3):
        image_stat_copy(r).start()
    for r in (1, 2, 3):
        image_stat_copy(r).wait_recv()

    def joined(parts):
        top = functools.reduce(jnp.maximum, [a[0:2] for a in parts])
        total = functools.reduce(jnp.add, [a[2:4] * jnp.exp(a[0:2] - top) for a in parts])
        return top, total

    top, total = joined([ist[0:4, :]] + [rist[r, 0:4, :] for r in range(3)])
    for which in (0, 1):
        asc[which] = jnp.exp(istat[which] - top[which : which + 1]) / total[which : which + 1]

    for i in range(6):
        text_stat_copy(i).wait_recv()
    for k in range(WINDOW):
        cols = pl.ds(k * ROWS, ROWS)
        parts = [tst[0:4, cols]]
        for i, shift in enumerate(SHIFTS):
            if 0 <= k + shift < WINDOW:
                parts.append(rts[i, 0:4, cols])
        top, total = joined(parts)
        tsct[0:2, cols] = jnp.exp(tst[0:2, cols] - top) / total
    tsc[...] = jnp.transpose(tsct[...])

    def weights(j):
        a_s, a_t = asc[0, pl.ds(j, 1), :], asc[1, pl.ds(j, 1), :]

        def slab(g, carry):
            rows = rows_of(j * CR + g * SLAB, SLAB)
            c_s, c_t = tsc[rows, 0:1], tsc[rows, 1:2]
            w[rows, :] = (
                e_img_s[rows, :] * a_s - e_img_t[rows, :] * a_t
                + e_txt_s[rows, :] * c_s - e_txt_t[rows, :] * c_t
            ).astype(BF16)
            return carry

        lax.fori_loop(0, CR // SLAB, slab, 0)

    def text_term(j):
        weights(j)
        return lax.dot_general(
            w[rows_of(j * CR, CR), :], img_s[...], NN, preferred_element_type=F32
        ) * scale_s

    def grad_copy(hop, c):
        rows = pl.ds(c * CR, CR)
        return remote(
            g_send.at[hop, rows], g_recv.at[hop, rows], g_ssem.at[hop, c], g_rsem.at[hop, c], at(1)
        )

    for c in range(CHUNKS):
        g_send[0, pl.ds(c * CR, CR), :] = text_term(3 * CHUNKS + c)
        grad_copy(0, c).start()

    def earlier(j, carry):
        p_own[rows_of(j * CR, CR), :] = text_term(j)
        return carry

    lax.fori_loop(0, 3 * CHUNKS, earlier, 0)

    def image_term(quarter):
        return lax.dot_general(
            w[:, rows_of(quarter * ROWS, ROWS)], txt_s[...], TN, preferred_element_type=F32
        ) * scale_s

    order = (sib, diag, far, p)

    def sib_copy(i):
        return remote(gi.at[i], gi_sib.at[i], gi_ssem.at[i], gi_rsem.at[i], (d, sib))

    for i in (1, 0):
        gi[i] = image_term(order[i])
        sib_copy(i).start()
    for i in (2, 3):
        gi[i] = image_term(order[i])
    sib_copy(1).wait_recv()
    gi_sum[...] = gi[2] + gi_sib[1]
    far_copy = remote(gi_sum, gi_x, gi_ssem.at[2], gi_rsem.at[2], (d, far))
    far_copy.start()

    for hop in range(3):
        for c in range(CHUNKS):
            rows = pl.ds(c * CR, CR)
            mine = p_own[pl.ds((2 - hop) * ROWS + c * CR, CR), :]
            grad_copy(hop, c).wait_recv()
            if hop < 2:
                g_send[hop + 1, rows, :] = mine + g_recv[hop, rows, :]
                grad_copy(hop + 1, c).start()
            else:
                out_text[rows, :] = mine + g_recv[hop, rows, :]
        if hop == 1:
            sib_copy(0).wait_recv()
            far_copy.wait_recv()
            out_image[...] = gi[3] + gi_sib[0] + gi_x[...]

    for n in range(3 * CHUNKS):
        for copy in text_copies(n):
            copy.wait_send()
    for copy in to_far + to_sib + pass_on:
        copy.wait_send()
    for i in range(6):
        text_stat_copy(i).wait_send()
    for r in (1, 2, 3):
        image_stat_copy(r).wait_send()
    for hop in range(3):
        for c in range(CHUNKS):
            grad_copy(hop, c).wait_send()
    for i in (0, 1):
        sib_copy(i).wait_send()
    far_copy.wait_send()


def on_device(groups, student_image, student_text, teacher_image, teacher_text):
    ds, dt = student_image.shape[1], teacher_image.shape[1]
    dma = pltpu.SemaphoreType.DMA
    vmem = pltpu.VMEM
    return pl.pallas_call(
        functools.partial(kernel, groups, 2.0 / math.sqrt(ds), 2.0 / math.sqrt(dt)),
        out_shape=(
            jax.ShapeDtypeStruct((ROWS, ds), F32),
            jax.ShapeDtypeStruct((ROWS, ds), F32),
        ),
        in_specs=[pl.BlockSpec(memory_space=pl.ANY)] * 4,
        out_specs=(pl.BlockSpec(memory_space=pltpu.VMEM),) * 2,
        scratch_shapes=[
            vmem((BLOCK, ds), BF16), vmem((BLOCK, dt), BF16),
            vmem((BLOCK, ds), BF16), vmem((BLOCK, dt), BF16),
            vmem((CR, BLOCK), F32), vmem((CR, BLOCK), F32),
            vmem((BLOCK, BLOCK), F32), vmem((BLOCK, BLOCK), F32),
            vmem((BLOCK, BLOCK), F32), vmem((BLOCK, BLOCK), F32),
            vmem((BLOCK, BLOCK), BF16),
            vmem((4, TILES, BLOCK), F32), vmem((8, BLOCK), F32), vmem((3, 8, BLOCK), F32),
            vmem((BLOCK, 128), F32), vmem((8, BLOCK), F32), vmem((6, 8, BLOCK), F32),
            vmem((128, BLOCK), F32), vmem((BLOCK, 128), F32), vmem((2, TILES, BLOCK), F32),
            vmem((3, ROWS, ds), F32), vmem((3, ROWS, ds), F32), vmem((3 * ROWS, ds), F32),
            vmem((4, ROWS, ds), F32), vmem((2, ROWS, ds), F32),
            vmem((ROWS, ds), F32), vmem((ROWS, ds), F32),
            dma((4,)), dma((2, 3 * CHUNKS)), dma((2, 3 * CHUNKS)), dma((2, 3)), dma((2, 3)),
            dma((6,)), dma((6,)), dma((3,)), dma((3,)),
            dma((3, CHUNKS)), dma((3, CHUNKS)), dma((3,)), dma((3,)),
        ],
        compiler_params=pltpu.CompilerParams(
            collective_id=0, has_side_effects=True, vmem_limit_bytes=56 * 2**20
        ),
    )(student_image, student_text, teacher_image, teacher_text)


def solution(mesh):
    spec = P(("dp", "pair"), None)
    return jax.shard_map(
        functools.partial(on_device, mesh.shape["dp"]),
        mesh=mesh,
        in_specs=(spec,) * 4,
        out_specs=(spec, spec),
        check_vma=False,
    )
```

time: 926 us -> 181 us (0.20)
  waiting for transfers between devices: 817 us -> 0 us
  Pallas kernels: 0 us -> 178 us
  blocking collectives: 27.9 us -> 0 us
  starting transfers between devices: 26.6 us -> 0 us
  other arithmetic: 17.7 us -> 0 us
  between operations: 14.3 us -> 0.65 us
  matrix products: 9.95 us -> 0 us
  local copies, waits for them, and re-layouts: 12.4 us -> 2.72 us
    ppermute x12 -> x0, waiting for transfers between devices: 739 us -> none  [from_behind(): return lax.ppermute(value, axis, pairs)]
    pallas_call x0 -> x1, Pallas kernels: none -> 178 us  [on_device(): pl.pallas_call(functools.partial(kernel, groups, 2.0 / math.sqrt(ds), 2.0...]
    all_gather x1 -> x0, waiting for transfers between devices: 42.7 us -> none  [on_device(): own_block = lax.all_gather(both_text, 'pair', axis=0, tiled=True)]
    reduce_scatter x1 -> x0, waiting for transfers between devices: 35 us -> none  [on_device(): lax.psum_scatter(text_home, 'pair', scatter_dimension=0, tiled=True)]
    all_gather x4 -> x0, blocking collectives: 27.9 us -> none  [combined_all(): pieces = jax.tree.map(lambda part: lax.all_gather(part, axis), value)]
    ppermute x12 -> x0, starting transfers between devices: 26.5 us -> none  [from_behind(): return lax.ppermute(value, axis, pairs)]
    dot_general x4 -> x0, matrix products: 9.95 us -> none  [the longest x1 4.31 us: on_device(): image_terms = jnp.dot(weights, part_s, preferred_element_type=jnp.float32)]
  transfers between devices with their start and end apart: 14 -> 0, of which waited for: 12 -> 0; matrix products, arithmetic and copies ran while one was open for 1% -> 0% of each run, Pallas kernels for 0% -> 0%
where the time goes in v1:
time: 181 us
  Pallas kernels  178 us (98%)
  local copies, waits for them, and re-layouts  2.72 us (2%)
    pallas_call x1, Pallas kernels, on_device(): pl.pallas_call(functools.partial(kernel, groups, 2.0 / math.sqrt(ds), 2.0...  178 us

profile of v1, /device:TPU:1, one launch (start us, length us, event | category | flops | bytes accessed | tf_op | source)
XLA Modules:
  0.0 181.0 jit_solution(16478211561889969367)
XLA Ops:
  0.6 177.7 %shard_map.59 = (f32[256,512]{1,0:T(8,128)}, f32[256,512]{1,0:T(8,128)}) custom-call(bf16[256,512]{1,0:T(8,128)(2,1)} %si.1, bf16[256,512]{1,0:T(8,128)(2,1)} %st.1, bf16[256,1280]{1,0:T(8,128)(2,1)} %ti.1, bf16[256,1280]{1,0:T(8,128)(2,1)} %tt.1), custom_call_target="tpu_custom_call" | custom-call | tf_op jit(solution)/shard_map/pallas_call | solution.py:306
  178.3 0.0 copy-start
  178.3 1.9 %copy.8 = f32[256,512]{1,0:T(8,128)} copy(f32[256,512]{1,0:T(8,128)} %get-tuple-element.4) | data formatting | bytes 1048576
  180.3 0.0 copy-done
  180.3 0.8 copy.9
Async XLA Ops:
  178.3 1.9 %copy-start = (f32[256,512]{1,0:T(8,128)S(1)}, f32[256,512]{1,0:T(8,128)}, u32[]{:S(2)}) copy-start(f32[256,512]{1,0:T(8,128)} %get-tuple-element.5) | copy-start | bytes 1572868

commit v2 on v1

--- a/solution.py
+++ b/solution.py
@@ -21,13 +21,38 @@
 TILES = WINDOW * CHUNKS
 SLAB = 32
 SHIFTS = (-3, -2, -1, 1, 2, 3)
+LINE = 8
+PIECES = 4
 NT = (((1,), (1,)), ((), ()))
 NN = (((1,), (0,)), ((), ()))
 TN = (((0,), (0,)), ((), ()))
 
 
+SPAN, LOW = 240.0 * math.log(2.0), 120.0 * math.log(2.0)
+
+
 def rows_of(start, size):
     return pl.ds(pl.multiple_of(start, size), size)
+
+
+def encoded(x):
+    rows, width = x.shape
+    parts = jnp.abs(x).reshape(rows // 8, 8, width)
+    top = jnp.max(parts, axis=0)
+    top = functools.reduce(jnp.maximum, [top[:, i : i + 128] for i in range(0, width, 128)])
+    top = jnp.maximum(top, 1e-36)
+    ratio = jnp.concatenate([SPAN / top] * (width // 128), axis=1)
+    size = jnp.exp(parts * ratio[None] - LOW).reshape(rows, width)
+    return jnp.where(x < 0, -size, size).astype(BF16), top
+
+
+def decoded(code, top):
+    rows, width = code.shape
+    y = code.astype(F32)
+    size = (jnp.log(jnp.abs(y)) + LOW).reshape(rows // 8, 8, width)
+    scale = jnp.concatenate([top * (1.0 / SPAN)] * (width // 128), axis=1)
+    x = (size * scale[None]).reshape(rows, width)
+    return jnp.where(y < 0, -x, x)
 
 
 def kernel(
@@ -36,7 +61,7 @@
     img_s, img_t, txt_s, txt_t,
     s_buf, t_buf, e_img_s, e_img_t, e_txt_s, e_txt_t, w,
     istat, ist, rist, tcol, tst, rts, tsct, tsc, asc,
-    g_send, g_recv, p_own, gi, gi_sib, gi_x, gi_sum,
+    g_send, g_recv, g_stop, g_rtop, p_own, gi, gi_sib, x_send, x_recv, x_stop, x_rtop,
     local_sem, tx_send, tx_recv, im_send, im_recv,
     ts_send, ts_recv, is_send, is_recv, g_ssem, g_rsem, gi_ssem, gi_rsem,
 ):
@@ -47,8 +72,15 @@
     diag = 3 - p
     mates = {1: sib, 2: far, 3: diag}
 
-    def at(shift):
-        return (lax.rem(d + shift + groups, groups), p)
+    place = lax.rem(d, LINE)
+    last = place == LINE - 1
+
+    def at(shift, c):
+        group = lax.rem(d + shift + groups, groups)
+        if c % 2 == 0:
+            return (group, p)
+        turns = jnp.logical_or(place + shift < 0, place + shift >= LINE)
+        return (group, jnp.where(turns, far, p))
 
     def remote(src, dst, ssem, rsem, device):
         return pltpu.make_async_remote_copy(
@@ -58,57 +90,82 @@
 
     own_rows = rows_of(p * ROWS, ROWS)
     locals_ = [
-        pltpu.make_async_copy(st, txt_s.at[pl.ds(0, ROWS)], local_sem.at[0]),
-        pltpu.make_async_copy(tt, txt_t.at[pl.ds(0, ROWS)], local_sem.at[1]),
-        pltpu.make_async_copy(si, img_s.at[own_rows], local_sem.at[2]),
-        pltpu.make_async_copy(ti, img_t.at[own_rows], local_sem.at[3]),
+        pltpu.make_async_copy(si, img_s.at[own_rows], local_sem.at[0]),
+        pltpu.make_async_copy(ti, img_t.at[own_rows], local_sem.at[1]),
     ]
+    for c in range(CHUNKS):
+        for i, (src, buf) in enumerate(((st, txt_s), (tt, txt_t))):
+            locals_.append(pltpu.make_async_copy(
+                src.at[pl.ds(c * CR, CR)], buf.at[pl.ds(c * WINDOW * CR, CR)], local_sem.at[2 + 2 * c + i]
+            ))
     for copy in locals_:
         copy.start()
 
     barrier = pltpu.get_barrier_semaphore()
     for shift in SHIFTS:
-        pl.semaphore_signal(barrier, inc=1, device_id=at(shift), device_id_type=MESH)
+        group = lax.rem(d + shift + groups, groups)
+        for other in (p, far):
+            pl.semaphore_signal(barrier, inc=1, device_id=(group, other), device_id_type=MESH)
     for r in (1, 2, 3):
         pl.semaphore_signal(barrier, inc=1, device_id=(d, mates[r]), device_id_type=MESH)
     for copy in locals_:
         copy.wait()
-    pl.semaphore_wait(barrier, 9)
-
-    def text_copies(n):
-        here, there = pl.ds(n * CR, CR), pl.ds((n + CHUNKS) * CR, CR)
+    pl.semaphore_wait(barrier, 15)
+
+    def text_copies(k, c):
+        here, there = pl.ds((c * WINDOW + k) * CR, CR), pl.ds((c * WINDOW + k + 1) * CR, CR)
         return [
-            remote(buf.at[here], buf.at[there], tx_send.at[i, n], tx_recv.at[i, n], at(-1))
+            remote(buf.at[here], buf.at[there], tx_send.at[i, k, c], tx_recv.at[i, k, c], at(-1, c))
             for i, buf in enumerate((txt_s, txt_t))
         ]
 
-    def send_text(n):
-        for copy in text_copies(n):
+    def send_text(k, c):
+        for copy in text_copies(k, c):
             copy.start()
 
-    def text_arrives(n):
-        for copy in text_copies(n - CHUNKS):
+    def text_arrives(k, c):
+        for copy in text_copies(k - 1, c):
             copy.wait_recv()
 
-    def image_copies(slot, quarter, device):
-        rows = rows_of(quarter * ROWS, ROWS)
+    def image_copies(slot, start, size, device):
+        rows = rows_of(start, size)
         return [
             remote(buf.at[rows], buf.at[rows], im_send.at[i, slot], im_recv.at[i, slot], device)
             for i, buf in enumerate((img_s, img_t))
         ]
 
-    to_far = image_copies(0, p, (d, far))
-    to_sib = image_copies(1, p, (d, sib))
-    pass_on = image_copies(2, far, (d, sib))
-    for copy in to_far + to_sib:
+    size = ROWS // PIECES
+    to_far = [image_copies(2 + i, p * ROWS + i * size, size, (d, far)) for i in range(PIECES)]
+    to_sib = image_copies(0, p * ROWS, ROWS, (d, sib))
+    pass_on = image_copies(1, far * ROWS, ROWS, (d, sib))
+
+    def send_far(i):
+        for copy in to_far[i]:
+            copy.start()
+
+    for copy in to_sib:
         copy.start()
-    for n in range(CHUNKS):
-        send_text(n)
-    for n in range(CHUNKS, 2 * CHUNKS):
-        text_arrives(n)
-        send_text(n)
-    for copy in to_far:
-        copy.wait_recv()
+    send_text(0, 0)
+    send_far(0)
+    for c in range(1, CHUNKS):
+        send_text(0, c)
+
+    @pl.when(jnp.logical_not(last))
+    def _():
+        for i in range(1, PIECES):
+            send_far(i)
+
+    early = [(1, c) for c in range(CHUNKS)] + [(2, c) for c in range(CHUNKS - 1)]
+    for i, (k, c) in enumerate(early):
+        text_arrives(k, c)
+        send_text(k, c)
+        if i + 1 < PIECES:
+            @pl.when(last)
+            def _(i=i):
+                send_far(i + 1)
+    for piece in to_far:
+        for copy in piece:
+            copy.wait_recv()
     for copy in pass_on:
         copy.start()
     for copy in to_sib + pass_on:
@@ -143,16 +200,18 @@
         istat[which, pl.ds(j, 1), :] = top
         istat[which + 2, pl.ds(j, 1), :] = jnp.sum(total, axis=0, keepdims=True)
 
-    def tile(j, carry):
-        for n in range(2 * CHUNKS, 3 * CHUNKS):
-            @pl.when(j == 2 * (n - 2 * CHUNKS + 1))
+    def tile(step, carry):
+        k, c = step // CHUNKS, lax.rem(step, CHUNKS)
+        j = c * WINDOW + k
+        for n in range(CHUNKS):
+            if n == CHUNKS - 1:
+                @pl.when(step == CHUNKS)
+                def _():
+                    text_arrives(2, n)
+                    send_text(2, n)
+            @pl.when(step == 3 * CHUNKS + n)
             def _(n=n):
-                text_arrives(n)
-                send_text(n)
-        for n in range(3 * CHUNKS, 4 * CHUNKS):
-            @pl.when(j == n)
-            def _(n=n):
-                text_arrives(n)
+                text_arrives(3, n)
         rows = rows_of(j * CR, CR)
         s_buf[...] = lax.dot_general(txt_s[rows, :], img_s[...], NT, preferred_element_type=F32) * scale_s
         t_buf[...] = lax.dot_general(txt_t[rows, :], img_t[...], NT, preferred_element_type=F32) * scale_t
@@ -164,17 +223,19 @@
 
     tst[...] = jnp.transpose(tcol[...])[0:8, :]
 
-    def text_stat_copy(i):
+    def text_stat_copy(i, c):
         shift = SHIFTS[i]
         low, high = max(0, shift), min(WINDOW, WINDOW + shift)
-        size = (high - low) * ROWS
+        size = (high - low) * CR
+        here, there = (c * WINDOW + low) * CR, (c * WINDOW + low - shift) * CR
         return remote(
-            tst.at[:, pl.ds(low * ROWS, size)], rts.at[i, :, pl.ds((low - shift) * ROWS, size)],
-            ts_send.at[i], ts_recv.at[i], at(shift),
+            tst.at[:, pl.ds(here, size)], rts.at[i, :, pl.ds(there, size)],
+            ts_send.at[i, c], ts_recv.at[i, c], at(shift, c),
         )
 
-    for i in range(6):
-        text_stat_copy(i).start()
+    text_stat_copies = [text_stat_copy(i, c) for i in range(6) for c in range(CHUNKS)]
+    for copy in text_stat_copies:
+        copy.start()
 
     for which in (0, 1):
         tops, totals = istat[which], istat[which + 2]
@@ -199,13 +260,13 @@
     for which in (0, 1):
         asc[which] = jnp.exp(istat[which] - top[which : which + 1]) / total[which : which + 1]
 
-    for i in range(6):
-        text_stat_copy(i).wait_recv()
-    for k in range(WINDOW):
-        cols = pl.ds(k * ROWS, ROWS)
+    for copy in text_stat_copies:
+        copy.wait_recv()
+    for j in range(TILES):
+        cols = pl.ds(j * CR, CR)
         parts = [tst[0:4, cols]]
         for i, shift in enumerate(SHIFTS):
-            if 0 <= k + shift < WINDOW:
+            if 0 <= j % WINDOW + shift < WINDOW:
                 parts.append(rts[i, 0:4, cols])
         top, total = joined(parts)
         tsct[0:2, cols] = jnp.exp(tst[0:2, cols] - top) / total
@@ -231,17 +292,23 @@
             w[rows_of(j * CR, CR), :], img_s[...], NN, preferred_element_type=F32
         ) * scale_s
 
-    def grad_copy(hop, c):
+    def grad_copies(hop, c):
         rows = pl.ds(c * CR, CR)
-        return remote(
-            g_send.at[hop, rows], g_recv.at[hop, rows], g_ssem.at[hop, c], g_rsem.at[hop, c], at(1)
-        )
+        return [
+            remote(g_send.at[hop, rows], g_recv.at[hop, rows], g_ssem.at[hop, c, 0], g_rsem.at[hop, c, 0], at(1, c)),
+            remote(g_stop.at[hop, c], g_rtop.at[hop, c], g_ssem.at[hop, c, 1], g_rsem.at[hop, c, 1], at(1, c)),
+        ]
+
+    def send_grad(hop, c, value):
+        g_send[hop, pl.ds(c * CR, CR), :], g_stop[hop, c] = encoded(value)
+        for copy in grad_copies(hop, c):
+            copy.start()
 
     for c in range(CHUNKS):
-        g_send[0, pl.ds(c * CR, CR), :] = text_term(3 * CHUNKS + c)
-        grad_copy(0, c).start()
-
-    def earlier(j, carry):
+        send_grad(0, c, text_term(c * WINDOW + 3))
+
+    def earlier(n, carry):
+        j = lax.rem(n, CHUNKS) * WINDOW + 2 - n // CHUNKS
         p_own[rows_of(j * CR, CR), :] = text_term(j)
         return carry
 
@@ -263,40 +330,41 @@
     for i in (2, 3):
         gi[i] = image_term(order[i])
     sib_copy(1).wait_recv()
-    gi_sum[...] = gi[2] + gi_sib[1]
-    far_copy = remote(gi_sum, gi_x, gi_ssem.at[2], gi_rsem.at[2], (d, far))
-    far_copy.start()
+    far_copies = [
+        remote(x_send, x_recv, gi_ssem.at[2], gi_rsem.at[2], (d, far)),
+        remote(x_stop, x_rtop, gi_ssem.at[3], gi_rsem.at[3], (d, far)),
+    ]
+    x_send[...], x_stop[...] = encoded(gi[2] + gi_sib[1])
+    for copy in far_copies:
+        copy.start()
 
     for hop in range(3):
         for c in range(CHUNKS):
             rows = pl.ds(c * CR, CR)
-            mine = p_own[pl.ds((2 - hop) * ROWS + c * CR, CR), :]
-            grad_copy(hop, c).wait_recv()
+            mine = p_own[pl.ds((c * WINDOW + 2 - hop) * CR, CR), :]
+            for copy in grad_copies(hop, c):
+                copy.wait_recv()
+            value = mine + decoded(g_recv[hop, rows, :], g_rtop[hop, c])
             if hop < 2:
-                g_send[hop + 1, rows, :] = mine + g_recv[hop, rows, :]
-                grad_copy(hop + 1, c).start()
+                send_grad(hop + 1, c, value)
             else:
-                out_text[rows, :] = mine + g_recv[hop, rows, :]
+                out_text[rows, :] = value
         if hop == 1:
             sib_copy(0).wait_recv()
-            far_copy.wait_recv()
-            out_image[...] = gi[3] + gi_sib[0] + gi_x[...]
-
-    for n in range(3 * CHUNKS):
-        for copy in text_copies(n):
-            copy.wait_send()
-    for copy in to_far + to_sib + pass_on:
+            for copy in far_copies:
+                copy.wait_recv()
+            out_image[...] = gi[3] + gi_sib[0] + decoded(x_recv[...], x_rtop[...])
+
+    for k in range(3):
+        for c in range(CHUNKS):
+            for copy in text_copies(k, c) + grad_copies(k, c):
+                copy.wait_send()
+    for copy in to_sib + pass_on + sum(to_far, []) + text_stat_copies + far_copies:
         copy.wait_send()
-    for i in range(6):
-        text_stat_copy(i).wait_send()
     for r in (1, 2, 3):
         image_stat_copy(r).wait_send()
-    for hop in range(3):
-        for c in range(CHUNKS):
-            grad_copy(hop, c).wait_send()
     for i in (0, 1):
         sib_copy(i).wait_send()
-    far_copy.wait_send()
 
 
 def on_device(groups, student_image, student_text, teacher_image, teacher_text):
@@ -321,12 +389,14 @@
             vmem((4, TILES, BLOCK), F32), vmem((8, BLOCK), F32), vmem((3, 8, BLOCK), F32),
             vmem((BLOCK, 128), F32), vmem((8, BLOCK), F32), vmem((6, 8, BLOCK), F32),
             vmem((128, BLOCK), F32), vmem((BLOCK, 128), F32), vmem((2, TILES, BLOCK), F32),
-            vmem((3, ROWS, ds), F32), vmem((3, ROWS, ds), F32), vmem((3 * ROWS, ds), F32),
-            vmem((4, ROWS, ds), F32), vmem((2, ROWS, ds), F32),
-            vmem((ROWS, ds), F32), vmem((ROWS, ds), F32),
-            dma((4,)), dma((2, 3 * CHUNKS)), dma((2, 3 * CHUNKS)), dma((2, 3)), dma((2, 3)),
-            dma((6,)), dma((6,)), dma((3,)), dma((3,)),
-            dma((3, CHUNKS)), dma((3, CHUNKS)), dma((3,)), dma((3,)),
+            vmem((3, ROWS, ds), BF16), vmem((3, ROWS, ds), BF16),
+            vmem((3, CHUNKS, 8, 128), F32), vmem((3, CHUNKS, 8, 128), F32),
+            vmem((BLOCK, ds), F32), vmem((4, ROWS, ds), F32), vmem((2, ROWS, ds), F32),
+            vmem((ROWS, ds), BF16), vmem((ROWS, ds), BF16), vmem((8, 128), F32), vmem((8, 128), F32),
+            dma((2 + 2 * CHUNKS,)), dma((2, 3, CHUNKS)), dma((2, 3, CHUNKS)),
+            dma((2, 2 + PIECES)), dma((2, 2 + PIECES)),
+            dma((6, CHUNKS)), dma((6, CHUNKS)), dma((3,)), dma((3,)),
+            dma((3, CHUNKS, 2)), dma((3, CHUNKS, 2)), dma((4,)), dma((4,)),
         ],
         compiler_params=pltpu.CompilerParams(
             collective_id=0, has_side_effects=True, vmem_limit_bytes=56 * 2**20

time: 181 us -> 137 us (0.76)
  Pallas kernels: 178 us -> 133 us
    pallas_call x1, Pallas kernels: 178 us -> 133 us  [on_device(): pl.pallas_call(functools.partial(kernel, groups, 2.0 / math.sqrt(ds), 2.0...]
where the time goes in v2:
time: 137 us; the launch traced here: 136 us
  Pallas kernels  133 us (97%)
  local copies, waits for them, and re-layouts  2.72 us (2%)
    pallas_call x1, Pallas kernels, on_device(): pl.pallas_call(functools.partial(kernel, groups, 2.0 / math.sqrt(ds), 2.0...  133 us

profile of v2, /device:TPU:1, one launch (start us, length us, event | category | flops | bytes accessed | tf_op | source)
XLA Modules:
  0.0 136.4 jit_solution(17596808409969292894)
XLA Ops:
  0.6 133.0 %shard_map.59 = (f32[256,512]{1,0:T(8,128)}, f32[256,512]{1,0:T(8,128)}) custom-call(bf16[256,512]{1,0:T(8,128)(2,1)} %si.1, bf16[256,512]{1,0:T(8,128)(2,1)} %st.1, bf16[256,1280]{1,0:T(8,128)(2,1)} %ti.1, bf16[256,1280]{1,0:T(8,128)(2,1)} %tt.1), custom_call_target="tpu_custom_call" | custom-call | tf_op jit(solution)/shard_map/pallas_call | solution.py:374
  133.7 0.0 copy-start
  133.7 1.9 %copy.8 = f32[256,512]{1,0:T(8,128)} copy(f32[256,512]{1,0:T(8,128)} %get-tuple-element.4) | data formatting | bytes 1048576
  135.6 0.0 copy-done
  135.6 0.8 copy.9
Async XLA Ops:
  133.7 1.9 %copy-start = (f32[256,512]{1,0:T(8,128)S(1)}, f32[256,512]{1,0:T(8,128)}, u32[]{:S(2)}) copy-start(f32[256,512]{1,0:T(8,128)} %get-tuple-element.5) | copy-start | bytes 1572868

commit v3 on v2

--- a/solution.py
+++ b/solution.py
@@ -77,10 +77,9 @@
 
     def at(shift, c):
         group = lax.rem(d + shift + groups, groups)
-        if c % 2 == 0:
-            return (group, p)
         turns = jnp.logical_or(place + shift < 0, place + shift >= LINE)
-        return (group, jnp.where(turns, far, p))
+        changes = jnp.logical_and(turns, lax.rem(p + c, 2) == 1)
+        return (group, jnp.where(changes, far, p))
 
     def remote(src, dst, ssem, rsem, device):
         return pltpu.make_async_remote_copy(
@@ -150,19 +149,13 @@
     for c in range(1, CHUNKS):
         send_text(0, c)
 
-    @pl.when(jnp.logical_not(last))
-    def _():
-        for i in range(1, PIECES):
-            send_far(i)
+    for i in range(1, PIECES):
+        send_far(i)
 
     early = [(1, c) for c in range(CHUNKS)] + [(2, c) for c in range(CHUNKS - 1)]
     for i, (k, c) in enumerate(early):
         text_arrives(k, c)
         send_text(k, c)
-        if i + 1 < PIECES:
-            @pl.when(last)
-            def _(i=i):
-                send_far(i + 1)
     for piece in to_far:
         for copy in piece:
             copy.wait_recv()

time: 137 us -> 115 us (0.84)
  Pallas kernels: 133 us -> 112 us
    pallas_call x1, Pallas kernels: 133 us -> 112 us  [on_device(): pl.pallas_call(functools.partial(kernel, groups, 2.0 / math.sqrt(ds), 2.0...]
where the time goes in v3:
time: 115 us
  Pallas kernels  112 us (97%)
  local copies, waits for them, and re-layouts  2.72 us (2%)
    pallas_call x1, Pallas kernels, on_device(): pl.pallas_call(functools.partial(kernel, groups, 2.0 / math.sqrt(ds), 2.0...  112 us
    unnamed x4, local copies, waits for them, and re-layouts  2.72 us

profile of v3, /device:TPU:1, one launch (start us, length us, event | category | flops | bytes accessed | tf_op | source)
XLA Modules:
  0.0 115.1 jit_solution(3072332300183948937)
XLA Ops:
  0.6 111.8 %shard_map.59 = (f32[256,512]{1,0:T(8,128)}, f32[256,512]{1,0:T(8,128)}) custom-call(bf16[256,512]{1,0:T(8,128)(2,1)} %si.1, bf16[256,512]{1,0:T(8,128)(2,1)} %st.1, bf16[256,1280]{1,0:T(8,128)(2,1)} %ti.1, bf16[256,1280]{1,0:T(8,128)(2,1)} %tt.1), custom_call_target="tpu_custom_call" | custom-call | tf_op jit(solution)/shard_map/pallas_call | solution.py:367
  112.4 0.0 copy-start
  112.4 1.9 %copy.8 = f32[256,512]{1,0:T(8,128)} copy(f32[256,512]{1,0:T(8,128)} %get-tuple-element.4) | data formatting | bytes 1048576
  114.3 0.0 copy-done
  114.3 0.8 copy.9
Async XLA Ops:
  112.4 1.9 %copy-start = (f32[256,512]{1,0:T(8,128)S(1)}, f32[256,512]{1,0:T(8,128)}, u32[]{:S(2)}) copy-start(f32[256,512]{1,0:T(8,128)} %get-tuple-element.5) | copy-start | bytes 1572868

commit v4 on v3

v4 whole, which is shorter than its diff:
```python
import functools
import math

import jax
import jax.numpy as jnp
from jax import lax
from jax.experimental import pallas as pl
from jax.experimental.pallas import tpu as pltpu
from jax.sharding import PartitionSpec as P

MESH = pl.DeviceIdType.MESH
F32 = jnp.float32
BF16 = jnp.bfloat16

WINDOW = 4
PAIR = 4
ROWS = 256
BLOCK = ROWS * PAIR
CHUNKS = 2
CR = ROWS // CHUNKS
TILES = WINDOW * CHUNKS
SLAB = 128
SHORT = 96
SHIFTS = (-3, -2, -1, 1, 2, 3)
LINE = 8
PIECES = 4
NT = (((1,), (1,)), ((), ()))
NN = (((1,), (0,)), ((), ()))
TN = (((0,), (0,)), ((), ()))


SPAN, LOW = 240.0 * math.log(2.0), 120.0 * math.log(2.0)


def rows_of(start, size):
    return pl.ds(pl.multiple_of(start, size), size)


def encoded(x):
    rows, width = x.shape
    parts = jnp.abs(x).reshape(rows // 8, 8, width)
    top = jnp.max(parts, axis=0)
    top = functools.reduce(jnp.maximum, [top[:, i : i + 128] for i in range(0, width, 128)])
    top = jnp.maximum(top, 1e-36)
    ratio = jnp.concatenate([SPAN / top] * (width // 128), axis=1)
    size = jnp.exp(parts * ratio[None] - LOW).reshape(rows, width)
    return jnp.where(x < 0, -size, size).astype(BF16), top


def decoded(code, top):
    rows, width = code.shape
    y = code.astype(F32)
    size = (jnp.log(jnp.abs(y)) + LOW).reshape(rows // 8, 8, width)
    scale = jnp.concatenate([top * (1.0 / SPAN)] * (width // 128), axis=1)
    x = (size * scale[None]).reshape(rows, width)
    return jnp.where(y < 0, -x, x)


def kernel(
    groups, scale_s, scale_t,
    si, st, ti, tt, out_image, out_text,
    img_s, img_t, txt_s, txt_t,
    s_buf, t_buf, e_img_s, e_img_t, e_txt_s, e_txt_t, w,
    istat, ist, rist, tcol, tst, rts, tsct, tsc, asc,
    relay_s, relay_t, g_send, g_recv, g_stop, g_rtop, p_own, gi, gi_sib, x_send, x_recv, x_stop, x_rtop,
    local_sem, tx_send, tx_recv, lw_send, lw_recv, im_send, im_recv,
    ts_send, ts_recv, is_send, is_recv, g_ssem, g_rsem, gi_ssem, gi_rsem,
):
    d = lax.axis_index("dp")
    p = lax.axis_index("pair")
    sib = p + 1 - 2 * lax.rem(p, 2)
    far = lax.rem(p + 2, PAIR)
    diag = 3 - p
    mates = {1: sib, 2: far, 3: diag}

    place = lax.rem(d, LINE)
    last = place == LINE - 1

    def at(shift, c):
        group = lax.rem(d + shift + groups, groups)
        turns = jnp.logical_or(place + shift < 0, place + shift >= LINE)
        changes = jnp.logical_and(turns, lax.rem(p + c, 2) == 1)
        return (group, jnp.where(changes, far, p))

    def round_line(shift):
        return d - place + lax.rem(place + shift, LINE)

    def remote(src, dst, ssem, rsem, device):
        return pltpu.make_async_remote_copy(
            src_ref=src, dst_ref=dst, send_sem=ssem, recv_sem=rsem,
            device_id=device, device_id_type=MESH,
        )

    own_rows = rows_of(p * ROWS, ROWS)
    locals_ = [
        pltpu.make_async_copy(si, img_s.at[own_rows], local_sem.at[0]),
        pltpu.make_async_copy(ti, img_t.at[own_rows], local_sem.at[1]),
    ]
    for c in range(CHUNKS):
        for i, (src, buf) in enumerate(((st, txt_s), (tt, txt_t))):
            locals_.append(pltpu.make_async_copy(
                src.at[pl.ds(c * CR, CR)], buf.at[pl.ds(c * WINDOW * CR, CR)], local_sem.at[2 + 2 * c + i]
            ))
    for copy in locals_:
        copy.start()

    barrier = pltpu.get_barrier_semaphore()
    for shift in SHIFTS:
        group = lax.rem(d + shift + groups, groups)
        for other in (p, far):
            pl.semaphore_signal(barrier, inc=1, device_id=(group, other), device_id_type=MESH)
    for shift in (-6, 6):
        group = lax.rem(d + shift + groups, groups)
        for other in (p, far):
            pl.semaphore_signal(barrier, inc=1, device_id=(group, other), device_id_type=MESH)
    for shift in (3, LINE - 3):
        pl.semaphore_signal(barrier, inc=1, device_id=(round_line(shift), p), device_id_type=MESH)
    for r in (1, 2, 3):
        pl.semaphore_signal(barrier, inc=1, device_id=(d, mates[r]), device_id_type=MESH)
    for copy in locals_:
        copy.wait()
    pl.semaphore_wait(barrier, 21)

    texts = ((txt_s, relay_s), (txt_t, relay_t))

    def text_copies(k, c):
        rows = SHORT if c else CR
        here, there = pl.ds((c * WINDOW + k) * CR, rows), pl.ds((c * WINDOW + k + 1) * CR, rows)
        return [
            remote(buf.at[here], buf.at[there], tx_send.at[i, k, c], tx_recv.at[i, k, c], at(-1, c))
            for i, (buf, _) in enumerate(texts)
        ]

    def long_copies(stage):
        def rows(k):
            return pl.ds((WINDOW + k) * CR + SHORT, CR - SHORT)

        if stage == 0:
            device = (round_line(3), p)
        elif stage == 1:
            group = lax.rem(d + jnp.where(place < 3, 2, -6) + groups, groups)
            turns = jnp.logical_and(place >= 3, place < 6)
            device = (group, jnp.where(jnp.logical_and(turns, lax.rem(p + 1, 2) == 1), far, p))
        else:
            device = at(1, 1)
        copies = []
        for i, (buf, relay) in enumerate(texts):
            src = (buf.at[rows(0)], relay, buf.at[rows(3)], buf.at[rows(2)])[stage]
            dst = (relay, buf.at[rows(3)], buf.at[rows(2)], buf.at[rows(1)])[stage]
            copies.append(remote(src, dst, lw_send.at[i, stage], lw_recv.at[i, stage], device))
        return copies

    def start(copies):
        for copy in copies:
            copy.start()

    def arrive(copies):
        for copy in copies:
            copy.wait_recv()

    def image_copies(slot, quarter, device, piece=0, pieces=1):
        rows = rows_of(quarter * ROWS + piece * (ROWS // pieces), ROWS // pieces)
        return [
            remote(buf.at[rows], buf.at[rows], im_send.at[i, slot], im_recv.at[i, slot], device)
            for i, buf in enumerate((img_s, img_t))
        ]

    far_pieces = [image_copies(2 + i, p, (d, far), i, PIECES) for i in range(PIECES)]
    to_far = sum(far_pieces, [])
    to_sib = image_copies(0, p, (d, sib))
    pass_on = image_copies(1, far, (d, sib))
    start(to_sib)
    start(text_copies(0, 0))
    start(far_pieces[0])
    start(long_copies(0))
    start(text_copies(0, 1))
    start(sum(far_pieces[1:], []))
    for c in range(CHUNKS):
        arrive(text_copies(0, c))
        start(text_copies(1, c))
    arrive(long_copies(0))
    start(long_copies(1))

    def more(n):
        if n < 2:
            arrive(text_copies(1, n))
            start(text_copies(2, n))
        else:
            arrive(long_copies(1))
            start(long_copies(2))

    for n in range(3):
        more(n)

    arrive(to_far)
    start(pass_on)
    arrive(to_sib + pass_on)

    tcol[...] = jnp.zeros_like(tcol)
    ist[...] = jnp.zeros_like(ist)
    tsct[...] = jnp.zeros_like(tsct)

    def tile_stats(j, count, buf, e_img, e_txt, which):
        base = j * CR

        def by_text(g, top):
            x = buf[rows_of(g * SLAB, SLAB), :]
            m = jnp.max(x, axis=1, keepdims=True)
            e = jnp.exp(x - m)
            rows = rows_of(base + g * SLAB, SLAB)
            e_txt[rows, :] = e
            tcol[rows, which : which + 1] = m
            tcol[rows, which + 2 : which + 3] = jnp.sum(e, axis=1, keepdims=True)
            return jnp.maximum(top, jnp.max(x.reshape(SLAB // 8, 8, BLOCK), axis=0))

        top = lax.fori_loop(0, count * CR // SLAB, by_text, jnp.full((8, BLOCK), -jnp.inf, F32))
        top = jnp.max(top, axis=0, keepdims=True)

        def by_image(g, total):
            e = jnp.exp(buf[rows_of(g * SLAB, SLAB), :] - top)
            e_img[rows_of(base + g * SLAB, SLAB), :] = e
            return total + jnp.sum(e.reshape(SLAB // 8, 8, BLOCK), axis=0)

        total = lax.fori_loop(0, count * CR // SLAB, by_image, jnp.zeros((8, BLOCK), F32))
        total = jnp.sum(total, axis=0, keepdims=True)
        for n in range(count):
            istat[which, j + n : j + n + 1, :] = top
            istat[which + 2, j + n : j + n + 1, :] = total if n == 0 else jnp.zeros_like(total)

    def text_stats(c):
        cols = pl.ds(c * WINDOW * CR, WINDOW * CR)
        tst[:, cols] = jnp.transpose(tcol[cols, :])[0:8, :]

    def text_stat_copies(c):
        copies = []
        for i, shift in enumerate(SHIFTS):
            low, high = max(0, shift), min(WINDOW, WINDOW + shift)
            size = (high - low) * CR
            here, there = (c * WINDOW + low) * CR, (c * WINDOW + low - shift) * CR
            copies.append(remote(
                tst.at[:, pl.ds(here, size)], rts.at[i, :, pl.ds(there, size)],
                ts_send.at[i, c], ts_recv.at[i, c], at(shift, c),
            ))
        return copies

    def tiles(j, count):
        rows = pl.ds(j * CR, count * CR)
        here = pl.ds(0, count * CR)
        s_buf[here, :] = lax.dot_general(txt_s[rows, :], img_s[...], NT, preferred_element_type=F32) * scale_s
        t_buf[here, :] = lax.dot_general(txt_t[rows, :], img_t[...], NT, preferred_element_type=F32) * scale_t
        tile_stats(j, count, s_buf, e_img_s, e_txt_s, 0)
        tile_stats(j, count, t_buf, e_img_t, e_txt_t, 1)

    tiles(0, 2)
    tiles(WINDOW, 1)
    tiles(2, 1)
    arrive(long_copies(2))
    start(long_copies(3))
    tiles(WINDOW + 2, 1)
    arrive(long_copies(3))
    tiles(WINDOW + 1, 1)
    arrive(text_copies(2, 0))
    tiles(3, 1)
    text_stats(0)
    start(text_stat_copies(0))
    arrive(text_copies(2, 1))
    tiles(WINDOW + 3, 1)

    for which in (0, 1):
        tops, totals = istat[which], istat[which + 2]
        top = jnp.max(tops, axis=0, keepdims=True)
        ist[which : which + 1, :] = top
        ist[which + 2 : which + 3, :] = jnp.sum(totals * jnp.exp(tops - top), axis=0, keepdims=True)

    def image_stat_copy(r):
        return remote(ist, rist.at[r - 1], is_send.at[r - 1], is_recv.at[r - 1], (d, mates[r]))

    image_stat_copies = [image_stat_copy(r) for r in (1, 2, 3)]
    start(image_stat_copies)
    text_stats(1)
    start(text_stat_copies(1))

    def joined(parts):
        top = functools.reduce(jnp.maximum, [a[0:2] for a in parts])
        total = functools.reduce(jnp.add, [a[2:4] * jnp.exp(a[0:2] - top) for a in parts])
        return top, total

    def text_scales(c):
        arrive(text_stat_copies(c))
        for k in range(WINDOW):
            cols = pl.ds((c * WINDOW + k) * CR, CR)
            parts = [tst[0:4, cols]]
            for i, shift in enumerate(SHIFTS):
                if 0 <= k + shift < WINDOW:
                    parts.append(rts[i, 0:4, cols])
            top, total = joined(parts)
            tsct[0:2, cols] = jnp.exp(tst[0:2, cols] - top) / total
        cols = pl.ds(c * WINDOW * CR, WINDOW * CR)
        tsc[cols, :] = jnp.transpose(tsct[:, cols])

    text_scales(0)
    arrive(image_stat_copies)
    top, total = joined([ist[0:4, :]] + [rist[r, 0:4, :] for r in range(3)])
    for which in (0, 1):
        asc[which] = jnp.exp(istat[which] - top[which : which + 1]) / total[which : which + 1]

    def weights(j):
        a_s, a_t = asc[0, pl.ds(j, 1), :], asc[1, pl.ds(j, 1), :]

        def slab(g, carry):
            rows = rows_of(j * CR + g * SLAB, SLAB)
            c_s, c_t = tsc[rows, 0:1], tsc[rows, 1:2]
            w[rows, :] = (
                e_img_s[rows, :] * a_s - e_img_t[rows, :] * a_t
                + e_txt_s[rows, :] * c_s - e_txt_t[rows, :] * c_t
            ).astype(BF16)
            return carry

        lax.fori_loop(0, CR // SLAB, slab, 0)

    def text_term(j):
        return lax.dot_general(
            w[rows_of(j * CR, CR), :], img_s[...], NN, preferred_element_type=F32
        ) * scale_s

    def grad_copies(hop, c):
        rows = pl.ds(c * CR, CR)
        return [
            remote(g_send.at[hop, rows], g_recv.at[hop, rows], g_ssem.at[hop, c, 0], g_rsem.at[hop, c, 0], at(1, c)),
            remote(g_stop.at[hop, c], g_rtop.at[hop, c], g_ssem.at[hop, c, 1], g_rsem.at[hop, c, 1], at(1, c)),
        ]

    def send_grad(hop, c, value):
        g_send[hop, pl.ds(c * CR, CR), :], g_stop[hop, c] = encoded(value)
        start(grad_copies(hop, c))

    def pass_grad(hop, c):
        rows = pl.ds(c * CR, CR)
        mine = p_own[pl.ds((c * WINDOW + 2 - hop) * CR, CR), :]
        arrive(grad_copies(hop, c))
        value = mine + decoded(g_recv[hop, rows, :], g_rtop[hop, c])
        if hop < 2:
            send_grad(hop + 1, c, value)
        else:
            out_text[rows, :] = value

    def own_terms(k):
        def one(c, carry):
            j = c * WINDOW + k
            p_own[rows_of(j * CR, CR), :] = text_term(j)
            return carry

        lax.fori_loop(0, CHUNKS, one, 0)

    def image_term(quarter):
        return lax.dot_general(
            w[:, rows_of(quarter * ROWS, ROWS)], txt_s[...], TN, preferred_element_type=F32
        ) * scale_s

    order = (sib, diag, far, p)
    sib_copies = [remote(gi.at[i], gi_sib.at[i], gi_ssem.at[i], gi_rsem.at[i], (d, sib)) for i in (0, 1)]
    far_copies = [
        remote(x_send, x_recv, gi_ssem.at[2], gi_rsem.at[2], (d, far)),
        remote(x_stop, x_rtop, gi_ssem.at[3], gi_rsem.at[3], (d, far)),
    ]

    weights(3)
    send_grad(0, 0, text_term(3))
    text_scales(1)
    weights(WINDOW + 3)
    send_grad(0, 1, text_term(WINDOW + 3))

    def other_weights(n, carry):
        weights(lax.rem(n, CHUNKS) * WINDOW + n // CHUNKS)
        return carry

    lax.fori_loop(0, 3 * CHUNKS, other_weights, 0)
    for i in (1, 0):
        gi[i] = image_term(order[i])
        sib_copies[i].start()
    own_terms(2)
    pass_grad(0, 0)
    gi[2] = image_term(order[2])
    arrive(sib_copies[1:])
    x_send[...], x_stop[...] = encoded(gi[2] + gi_sib[1])
    start(far_copies)
    pass_grad(0, 1)
    own_terms(1)
    gi[3] = image_term(order[3])
    pass_grad(1, 0)
    own_terms(0)
    pass_grad(1, 1)
    arrive(sib_copies[:1] + far_copies)
    out_image[...] = gi[3] + gi_sib[0] + decoded(x_recv[...], x_rtop[...])
    pass_grad(2, 0)
    pass_grad(2, 1)

    for k in range(3):
        for c in range(CHUNKS):
            for copy in text_copies(k, c) + grad_copies(k, c):
                copy.wait_send()
    for copies in [long_copies(n) for n in range(4)] + [text_stat_copies(c) for c in range(CHUNKS)]:
        for copy in copies:
            copy.wait_send()
    for copy in to_far + to_sib + pass_on + image_stat_copies + sib_copies + far_copies:
        copy.wait_send()


def on_device(groups, student_image, student_text, teacher_image, teacher_text):
    ds, dt = student_image.shape[1], teacher_image.shape[1]
    dma = pltpu.SemaphoreType.DMA
    vmem = pltpu.VMEM
    return pl.pallas_call(
        functools.partial(kernel, groups, 2.0 / math.sqrt(ds), 2.0 / math.sqrt(dt)),
        out_shape=(
            jax.ShapeDtypeStruct((ROWS, ds), F32),
            jax.ShapeDtypeStruct((ROWS, ds), F32),
        ),
        in_specs=[pl.BlockSpec(memory_space=pl.ANY)] * 4,
        out_specs=(pl.BlockSpec(memory_space=pltpu.VMEM),) * 2,
        scratch_shapes=[
            vmem((BLOCK, ds), BF16), vmem((BLOCK, dt), BF16),
            vmem((BLOCK, ds), BF16), vmem((BLOCK, dt), BF16),
            vmem((2 * CR, BLOCK), F32), vmem((2 * CR, BLOCK), F32),
            vmem((BLOCK, BLOCK), F32), vmem((BLOCK, BLOCK), F32),
            vmem((BLOCK, BLOCK), F32), vmem((BLOCK, BLOCK), F32),
            vmem((BLOCK, BLOCK), BF16),
            vmem((4, TILES, BLOCK), F32), vmem((8, BLOCK), F32), vmem((3, 8, BLOCK), F32),
            vmem((BLOCK, 128), F32), vmem((8, BLOCK), F32), vmem((6, 8, BLOCK), F32),
            vmem((128, BLOCK), F32), vmem((BLOCK, 128), F32), vmem((2, TILES, BLOCK), F32),
            vmem((CR - SHORT, ds), BF16), vmem((CR - SHORT, dt), BF16),
            vmem((3, ROWS, ds), BF16), vmem((3, ROWS, ds), BF16),
            vmem((3, CHUNKS, 8, 128), F32), vmem((3, CHUNKS, 8, 128), F32),
            vmem((BLOCK, ds), F32), vmem((4, ROWS, ds), F32), vmem((2, ROWS, ds), F32),
            vmem((ROWS, ds), BF16), vmem((ROWS, ds), BF16), vmem((8, 128), F32), vmem((8, 128), F32),
            dma((2 + 2 * CHUNKS,)), dma((2, 3, CHUNKS)), dma((2, 3, CHUNKS)),
            dma((2, 4)), dma((2, 4)), dma((2, 2 + PIECES)), dma((2, 2 + PIECES)),
            dma((6, CHUNKS)), dma((6, CHUNKS)), dma((3,)), dma((3,)),
            dma((3, CHUNKS, 2)), dma((3, CHUNKS, 2)), dma((4,)), dma((4,)),
        ],
        compiler_params=pltpu.CompilerParams(
            collective_id=0, has_side_effects=True, vmem_limit_bytes=56 * 2**20
        ),
    )(student_image, student_text, teacher_image, teacher_text)


def solution(mesh):
    spec = P(("dp", "pair"), None)
    return jax.shard_map(
        functools.partial(on_device, mesh.shape["dp"]),
        mesh=mesh,
        in_specs=(spec,) * 4,
        out_specs=(spec, spec),
        check_vma=False,
    )
```

time: 115 us -> 105 us (0.913)
  Pallas kernels: 112 us -> 101 us
    pallas_call x1, Pallas kernels: 112 us -> 101 us  [on_device(): pl.pallas_call(functools.partial(kernel, groups, 2.0 / math.sqrt(ds), 2.0...]
where the time goes in v4:
time: 105 us
  Pallas kernels  101 us (96%)
  local copies, waits for them, and re-layouts  2.72 us (3%)
    pallas_call x1, Pallas kernels, on_device(): pl.pallas_call(functools.partial(kernel, groups, 2.0 / math.sqrt(ds), 2.0...  101 us
    unnamed x4, local copies, waits for them, and re-layouts  2.72 us

profile of v4, /device:TPU:1, one launch (start us, length us, event | category | flops | bytes accessed | tf_op | source)
XLA Modules:
  0.0 104.9 jit_solution(16011395421864520397)
XLA Ops:
  0.6 101.5 %shard_map.59 = (f32[256,512]{1,0:T(8,128)}, f32[256,512]{1,0:T(8,128)}) custom-call(bf16[256,512]{1,0:T(8,128)(2,1)} %si.1, bf16[256,512]{1,0:T(8,128)(2,1)} %st.1, bf16[256,1280]{1,0:T(8,128)(2,1)} %ti.1, bf16[256,1280]{1,0:T(8,128)(2,1)} %tt.1), custom_call_target="tpu_custom_call" | custom-call | tf_op jit(solution)/shard_map/pallas_call | solution.py:413
  102.1 0.0 copy-start
  102.1 1.9 %copy.8 = f32[256,512]{1,0:T(8,128)} copy(f32[256,512]{1,0:T(8,128)} %get-tuple-element.4) | data formatting | bytes 1048576
  104.1 0.0 copy-done
  104.1 0.8 copy.9
Async XLA Ops:
  102.1 1.9 %copy-start = (f32[256,512]{1,0:T(8,128)S(1)}, f32[256,512]{1,0:T(8,128)}, u32[]{:S(2)}) copy-start(f32[256,512]{1,0:T(8,128)} %get-tuple-element.5) | copy-start | bytes 1572868

commit v5 on v4

--- a/solution.py
+++ b/solution.py
@@ -20,10 +20,11 @@
 CR = ROWS // CHUNKS
 TILES = WINDOW * CHUNKS
 SLAB = 128
-SHORT = 96
+SHORT = 64
 SHIFTS = (-3, -2, -1, 1, 2, 3)
 LINE = 8
 PIECES = 4
+PARTS = 2
 NT = (((1,), (1,)), ((), ()))
 NN = (((1,), (0,)), ((), ()))
 TN = (((0,), (0,)), ((), ()))
@@ -62,8 +63,8 @@
     img_s, img_t, txt_s, txt_t,
     s_buf, t_buf, e_img_s, e_img_t, e_txt_s, e_txt_t, w,
     istat, ist, rist, tcol, tst, rts, tsct, tsc, asc,
-    relay_s, relay_t, g_send, g_recv, g_stop, g_rtop, p_own, gi, gi_sib, x_send, x_recv, x_stop, x_rtop,
-    local_sem, tx_send, tx_recv, lw_send, lw_recv, im_send, im_recv,
+    relay_s, relay_t, corner_s, corner_t, g_send, g_recv, g_stop, g_rtop, p_own, gi, gi_sib, x_send, x_recv, x_stop, x_rtop,
+    local_sem, tx_send, tx_recv, cn_send, cn_recv, on_send, lw_send, lw_recv, im_send, im_recv,
     ts_send, ts_recv, is_send, is_recv, g_ssem, g_rsem, gi_ssem, gi_rsem,
 ):
     d = lax.axis_index("dp")
@@ -109,17 +110,20 @@
         group = lax.rem(d + shift + groups, groups)
         for other in (p, far):
             pl.semaphore_signal(barrier, inc=1, device_id=(group, other), device_id_type=MESH)
-    for shift in (-6, 6):
+    for shift in (-8, -6, 6, 8):
         group = lax.rem(d + shift + groups, groups)
         for other in (p, far):
             pl.semaphore_signal(barrier, inc=1, device_id=(group, other), device_id_type=MESH)
+    for shift in (-7, 7):
+        group = lax.rem(d + shift + groups, groups)
+        pl.semaphore_signal(barrier, inc=1, device_id=(group, p), device_id_type=MESH)
     for shift in (3, LINE - 3):
         pl.semaphore_signal(barrier, inc=1, device_id=(round_line(shift), p), device_id_type=MESH)
     for r in (1, 2, 3):
         pl.semaphore_signal(barrier, inc=1, device_id=(d, mates[r]), device_id_type=MESH)
     for copy in locals_:
         copy.wait()
-    pl.semaphore_wait(barrier, 21)
+    pl.semaphore_wait(barrier, 27)
 
     texts = ((txt_s, relay_s), (txt_t, relay_t))
 
@@ -131,9 +135,49 @@
             for i, (buf, _) in enumerate(texts)
         ]
 
-    def long_copies(stage):
+    corners = (corner_s, corner_t)
+    first = place == 0
+
+    def corner_copies(k):
+        here = pl.ds((WINDOW + k) * CR, SHORT)
+        device = (lax.rem(d - LINE + groups, groups), at(-1, 1)[1])
+        return [
+            remote(buf.at[here], held.at[k], cn_send.at[i, k], cn_recv.at[i, k], device)
+            for i, ((buf, _), held) in enumerate(zip(texts, corners))
+        ]
+
+    def onward_copies(k):
+        there = pl.ds((WINDOW + k + 1) * CR, SHORT)
+        device = (lax.rem(d + LINE - 1, groups), p)
+        return [
+            remote(held.at[k], buf.at[there], on_send.at[i, k], tx_recv.at[i, k, 1], device)
+            for i, ((buf, _), held) in enumerate(zip(texts, corners))
+        ]
+
+    def send_text(k, c):
+        if c == 0:
+            start(text_copies(k, 0))
+            return
+
+        @pl.when(first)
+        def _():
+            start(corner_copies(k))
+
+        @pl.when(jnp.logical_not(first))
+        def _():
+            start(text_copies(k, 1))
+
+    def corner_step(k):
+        @pl.when(first)
+        def _():
+            arrive(corner_copies(k))
+            start(onward_copies(k))
+
+    def long_copies(stage, part):
+        size = (CR - SHORT) // PARTS
+
         def rows(k):
-            return pl.ds((WINDOW + k) * CR + SHORT, CR - SHORT)
+            return pl.ds((WINDOW + k) * CR + SHORT + part * size, size)
 
         if stage == 0:
             device = (round_line(3), p)
@@ -145,9 +189,10 @@
             device = at(1, 1)
         copies = []
         for i, (buf, relay) in enumerate(texts):
-            src = (buf.at[rows(0)], relay, buf.at[rows(3)], buf.at[rows(2)])[stage]
-            dst = (relay, buf.at[rows(3)], buf.at[rows(2)], buf.at[rows(1)])[stage]
-            copies.append(remote(src, dst, lw_send.at[i, stage], lw_recv.at[i, stage], device))
+            between = relay.at[pl.ds(part * size, size)]
+            src = (buf.at[rows(0)], between, buf.at[rows(3)], buf.at[rows(2)])[stage]
+            dst = (between, buf.at[rows(3)], buf.at[rows(2)], buf.at[rows(1)])[stage]
+            copies.append(remote(src, dst, lw_send.at[i, stage, part], lw_recv.at[i, stage, part], device))
         return copies
 
     def start(copies):
@@ -170,27 +215,37 @@
     to_sib = image_copies(0, p, (d, sib))
     pass_on = image_copies(1, far, (d, sib))
     start(to_sib)
-    start(text_copies(0, 0))
+    send_text(0, 0)
+    start(long_copies(0, 0))
     start(far_pieces[0])
-    start(long_copies(0))
-    start(text_copies(0, 1))
+    for i in range(1, PARTS):
+        start(long_copies(0, i))
+    send_text(0, 1)
     start(sum(far_pieces[1:], []))
-    for c in range(CHUNKS):
-        arrive(text_copies(0, c))
-        start(text_copies(1, c))
-    arrive(long_copies(0))
-    start(long_copies(1))
-
-    def more(n):
-        if n < 2:
-            arrive(text_copies(1, n))
-            start(text_copies(2, n))
-        else:
-            arrive(long_copies(1))
-            start(long_copies(2))
-
-    for n in range(3):
-        more(n)
+
+    def text_step(k, c):
+        arrive(text_copies(k, c))
+        if k < 2:
+            send_text(k + 1, c)
+
+    def long_step(stage, part):
+        arrive(long_copies(stage, part))
+        if stage < 3:
+            start(long_copies(stage + 1, part))
+
+    long_step(0, 0)
+    corner_step(0)
+    text_step(0, 0)
+    text_step(0, 1)
+    long_step(0, 1)
+    long_step(1, 0)
+    corner_step(1)
+
+    @pl.when(last)
+    def _():
+        text_step(1, 0)
+        long_step(1, 1)
+        long_step(2, 0)
 
     arrive(to_far)
     start(pass_on)
@@ -252,19 +307,28 @@
         tile_stats(j, count, t_buf, e_img_t, e_txt_t, 1)
 
     tiles(0, 2)
-    tiles(WINDOW, 1)
+
+    @pl.when(jnp.logical_not(last))
+    def _():
+        text_step(1, 0)
+        long_step(1, 1)
+        long_step(2, 0)
+
+    tiles(4, 1)
+    text_step(1, 1)
+    long_step(2, 1)
     tiles(2, 1)
-    arrive(long_copies(2))
-    start(long_copies(3))
-    tiles(WINDOW + 2, 1)
-    arrive(long_copies(3))
-    tiles(WINDOW + 1, 1)
-    arrive(text_copies(2, 0))
+    corner_step(2)
+    tiles(6, 1)
+    long_step(3, 0)
+    long_step(3, 1)
+    tiles(5, 1)
+    text_step(2, 0)
     tiles(3, 1)
     text_stats(0)
     start(text_stat_copies(0))
-    arrive(text_copies(2, 1))
-    tiles(WINDOW + 3, 1)
+    text_step(2, 1)
+    tiles(7, 1)
 
     for which in (0, 1):
         tops, totals = istat[which], istat[which + 2]
@@ -395,11 +459,22 @@
     pass_grad(2, 0)
     pass_grad(2, 1)
 
+    @pl.when(first)
+    def _():
+        for k in range(3):
+            for copy in corner_copies(k) + onward_copies(k):
+                copy.wait_send()
+
+    @pl.when(jnp.logical_not(first))
+    def _():
+        for k in range(3):
+            for copy in text_copies(k, 1):
+                copy.wait_send()
+
     for k in range(3):
-        for c in range(CHUNKS):
-            for copy in text_copies(k, c) + grad_copies(k, c):
-                copy.wait_send()
-    for copies in [long_copies(n) for n in range(4)] + [text_stat_copies(c) for c in range(CHUNKS)]:
+        for copy in text_copies(k, 0) + grad_copies(k, 0) + grad_copies(k, 1):
+            copy.wait_send()
+    for copies in [long_copies(n, i) for n in range(4) for i in range(PARTS)] + [text_stat_copies(c) for c in range(CHUNKS)]:
         for copy in copies:
             copy.wait_send()
     for copy in to_far + to_sib + pass_on + image_stat_copies + sib_copies + far_copies:
@@ -410,11 +485,11 @@
     ds, dt = student_image.shape[1], teacher_image.shape[1]
     dma = pltpu.SemaphoreType.DMA
     vmem = pltpu.VMEM
-    return pl.pallas_call(
+    results = pl.pallas_call(
         functools.partial(kernel, groups, 2.0 / math.sqrt(ds), 2.0 / math.sqrt(dt)),
         out_shape=(
-            jax.ShapeDtypeStruct((ROWS, ds), F32),
-            jax.ShapeDtypeStruct((ROWS, ds), F32),
+            vmem((ROWS, ds), F32),
+            vmem((ROWS, ds), F32),
         ),
         in_specs=[pl.BlockSpec(memory_space=pl.ANY)] * 4,
         out_specs=(pl.BlockSpec(memory_space=pltpu.VMEM),) * 2,
@@ -429,12 +504,14 @@
             vmem((BLOCK, 128), F32), vmem((8, BLOCK), F32), vmem((6, 8, BLOCK), F32),
             vmem((128, BLOCK), F32), vmem((BLOCK, 128), F32), vmem((2, TILES, BLOCK), F32),
             vmem((CR - SHORT, ds), BF16), vmem((CR - SHORT, dt), BF16),
+            vmem((3, SHORT, ds), BF16), vmem((3, SHORT, dt), BF16),
             vmem((3, ROWS, ds), BF16), vmem((3, ROWS, ds), BF16),
             vmem((3, CHUNKS, 8, 128), F32), vmem((3, CHUNKS, 8, 128), F32),
             vmem((BLOCK, ds), F32), vmem((4, ROWS, ds), F32), vmem((2, ROWS, ds), F32),
             vmem((ROWS, ds), BF16), vmem((ROWS, ds), BF16), vmem((8, 128), F32), vmem((8, 128), F32),
             dma((2 + 2 * CHUNKS,)), dma((2, 3, CHUNKS)), dma((2, 3, CHUNKS)),
-            dma((2, 4)), dma((2, 4)), dma((2, 2 + PIECES)), dma((2, 2 + PIECES)),
+            dma((2, 3)), dma((2, 3)), dma((2, 3)),
+            dma((2, 4, PARTS)), dma((2, 4, PARTS)), dma((2, 2 + PIECES)), dma((2, 2 + PIECES)),
             dma((6, CHUNKS)), dma((6, CHUNKS)), dma((3,)), dma((3,)),
             dma((3, CHUNKS, 2)), dma((3, CHUNKS, 2)), dma((4,)), dma((4,)),
         ],
@@ -442,6 +519,7 @@
             collective_id=0, has_side_effects=True, vmem_limit_bytes=56 * 2**20
         ),
     )(student_image, student_text, teacher_image, teacher_text)
+    return tuple(results)
 
 
 def solution(mesh):

time: 105 us -> 93.2 us (0.89)
  Pallas kernels: 101 us -> 90.8 us
  local copies, waits for them, and re-layouts: 2.72 us -> 1.59 us
    pallas_call x1, Pallas kernels: 101 us -> 90.8 us  [on_device(): pl.pallas_call(functools.partial(kernel, groups, 2.0 / math.sqrt(ds), 2.0...]
    unnamed x4 -> x2, local copies, waits for them, and re-layouts: 2.72 us -> 1.59 us
where the time goes in v5:
time: 93.2 us; the launch traced here: 93 us
  Pallas kernels  90.8 us (97%)
  local copies, waits for them, and re-layouts  1.59 us (2%)
    pallas_call x1, Pallas kernels, on_device(): pl.pallas_call(functools.partial(kernel, groups, 2.0 / math.sqrt(ds), 2.0...  90.8 us

profile of v5, /device:TPU:1, one launch (start us, length us, event | category | flops | bytes accessed | tf_op | source)
XLA Modules:
  0.0 93.0 jit_solution(17463145456597653378)
XLA Ops:
  0.6 90.8 %shard_map.59 = (f32[256,512]{1,0:T(8,128)S(1)}, f32[256,512]{1,0:T(8,128)S(1)}) custom-call(bf16[256,512]{1,0:T(8,128)(2,1)} %si.1, bf16[256,512]{1,0:T(8,128)(2,1)} %st.1, bf16[256,1280]{1,0:T(8,128)(2,1)} %ti.1, bf16[256,1280]{1,0:T(8,128)(2,1)} %tt.1), custom_call_target="tpu_custom_call" | custom-call | tf_op jit(solution)/shard_map/pallas_call | solution.py:488
  91.4 0.8 copy.8
  92.2 0.8 copy.9
